TPU v7x, 256 devices: a whole 4x4x8 slice. The times are simulated.
256 devices in a mesh: heads: 4 (over y_lo, core), tokens: 64 (over x, z, y_hi).
Axes of the slice: x: 4, y: 4 (y_hi: 2, y_lo: 2; y = y_hi * 2 + y_lo), z: 8, core: 2. Of those that a mesh axis runs over, the one named last changes fastest.
Arguments:
- queries: bfloat16 [32768, 4096], P(('heads', 'tokens')), may hold values from -6 to 6
- keys: bfloat16 [32768, 4096], P(('heads', 'tokens')), may hold values from -6 to 6
- values: bfloat16 [32768, 4096], P(('heads', 'tokens')), may hold values from -6 to 6
- rates: float32 [32768, 8], P(('heads', 'tokens')), may hold values from 0.0003 to 0.003
- gate_fast: bfloat16 [8, 512, 512], P('heads'), may hold values from -0.25 to 0.25
- down_fast: bfloat16 [8, 512, 512], P('heads'), may hold values from -0.25 to 0.25
- up_fast: bfloat16 [8, 512, 512], P('heads'), may hold values from -0.25 to 0.25
Outputs:
- outputs: bfloat16 [32768, 4096], P(('heads', 'tokens'))
- gate_next: bfloat16 [8, 512, 512], P('heads')
- down_next: bfloat16 [8, 512, 512], P('heads')
- up_next: bfloat16 [8, 512, 512], P('heads')
All inputs are finite; a program needn't handle non-finite values.
Results may differ from a plain program's by a relative error of at most 0.025.
Values may be sent and summed in bfloat16 or wider, within the bound.
A program may use at most 64 MiB of HBM per device.

v0:
```python
import jax
import jax.numpy as jnp
from jax import lax
from jax.sharding import PartitionSpec as P


def inner_sum(left, right):
    return lax.dot_general(
        left, right, (((0,), (0,)), ((), ())), preferred_element_type=jnp.float32
    )


def renormed(weight, gradient):
    wide = weight.astype(jnp.float32)
    moved = wide - gradient
    factor = jnp.sqrt(jnp.sum(wide * wide, axis=1)) / jnp.sqrt(
        jnp.sum(moved * moved, axis=1) + 1e-06
    )
    return (moved * factor[:, None, :]).astype(jnp.bfloat16)


def shards(queries, keys, values, rates, gate_fast, down_fast, up_fast):
    query_rows, key_rows, value_rows, rate_rows = (
        lax.all_to_all(queries, "heads", split_axis=1, concat_axis=0, tiled=True),
        lax.all_to_all(keys, "heads", split_axis=1, concat_axis=0, tiled=True),
        lax.all_to_all(values, "heads", split_axis=1, concat_axis=0, tiled=True),
        lax.all_to_all(
            rates.astype(jnp.bfloat16), "heads", split_axis=1, concat_axis=0, tiled=True
        ).astype(rates.dtype),
    )
    heads_here = gate_fast.shape[0]
    width = gate_fast.shape[1]
    grads_gate = []
    grads_down = []
    grads_up = []
    for head in range(heads_here):
        cols = slice(head * width, (head + 1) * width)
        key_head = key_rows[:, cols]
        gate_pre = jnp.dot(key_head, gate_fast[head], preferred_element_type=jnp.float32)
        up_pre = jnp.dot(key_head, up_fast[head], preferred_element_type=jnp.float32)
        sigma = jax.nn.sigmoid(gate_pre)
        hidden = (gate_pre * sigma * up_pre).astype(jnp.bfloat16)
        d_out = (-rate_rows[:, head][:, None] * value_rows[:, cols].astype(jnp.float32)).astype(
            jnp.bfloat16
        )
        d_hidden = lax.dot_general(
            d_out, down_fast[head], (((1,), (1,)), ((), ())), preferred_element_type=jnp.float32
        )
        d_gate = (d_hidden * up_pre * sigma * (1.0 + gate_pre * (1.0 - sigma))).astype(jnp.bfloat16)
        d_up = (d_hidden * gate_pre * sigma).astype(jnp.bfloat16)
        grads_gate.append(inner_sum(key_head, d_gate))
        grads_down.append(inner_sum(hidden, d_out))
        grads_up.append(inner_sum(key_head, d_up))
    local_gate = jnp.stack(grads_gate)
    local_down = jnp.stack(grads_down)
    local_up = jnp.stack(grads_up)
    total_gate, total_down, total_up = lax.psum((local_gate, local_down, local_up), "tokens")
    gate_next = renormed(gate_fast, total_gate)
    down_next = renormed(down_fast, total_down)
    up_next = renormed(up_fast, total_up)
    results = []
    for head in range(heads_here):
        query_head = query_rows[:, head * width : (head + 1) * width]
        first = jnp.dot(query_head, gate_next[head], preferred_element_type=jnp.float32)
        second = jnp.dot(query_head, up_next[head], preferred_element_type=jnp.float32)
        mixed = (first * jax.nn.sigmoid(first) * second).astype(jnp.bfloat16)
        results.append(
            jnp.dot(mixed, down_next[head], preferred_element_type=jnp.float32).astype(jnp.bfloat16)
        )
    grouped = jnp.concatenate(results, axis=1)
    outputs = lax.all_to_all(grouped, "heads", split_axis=0, concat_axis=1, tiled=True)
    return (outputs, gate_next, down_next, up_next)


def solution(mesh):
    placed = (
        P(("heads", "tokens"), None),
        P(("heads", "tokens"), None),
        P(("heads", "tokens"), None),
        P(("heads", "tokens"), None),
        P("heads", None, None),
        P("heads", None, None),
        P("heads", None, None),
    )
    return jax.shard_map(
        shards,
        mesh=mesh,
        in_specs=placed,
        out_specs=(
            P(("heads", "tokens"), None),
            P("heads", None, None),
            P("heads", None, None),
            P("heads", None, None),
        ),
        check_vma=False,
    )
```

profile of v0, /device:TPU:1, one launch (start us, length us, event | category | flops | bytes accessed | tf_op | source)
XLA Modules:
  0.0 834.4 jit_solution(7082363922646221432)
XLA Ops:
  8.4 6.4 all-to-all-start
  14.9 2.3 copy.45
  17.8 4.2 all-to-all-start.2
  23.3 12.3 %all-to-all-done.2 = bf16[128,4,1024]{0,2,1:T(8,128)(2,1)S(1)} async-done(((bf16[128,4,1024]{0,2,1:T(8,128)(2,1)}), bf16[128,4,1024]{0,2,1:T(8,128)(2,1)S(1)}, u32[]{:S(2)}, u32[]{:S(2)}) %all-to-all-start.2) | async-done | bytes 1048608 | tf_op jit(solution)/shard_map/all_to_all | solution.py:25
  35.6 4.4 all-to-all-start.1
  40.5 2.6 fusion.23
  43.1 1.4 fusion.17
  44.5 1.4 fusion.25
  46.0 1.4 fusion.19
  47.4 6.2 all-to-all-done.1
  53.6 1.3 copy.44
  54.9 1.6 fusion.21
  63.5 1.5 pad_maximum_fusion
  65.0 1.5 pad_maximum_fusion.1
  66.5 1.5 pad_maximum_fusion.2
  70.6 4.4 all-to-all-start.3
  75.5 1.5 copy.50
  77.0 15.4 %all-to-all-done.3 = bf16[128,4,1024]{0,2,1:T(8,128)(2,1)S(1)} async-done(((bf16[128,4,1024]{0,2,1:T(8,128)(2,1)}), bf16[128,4,1024]{0,2,1:T(8,128)(2,1)S(1)}, u32[]{:S(2)}, u32[]{:S(2)}) %all-to-all-start.3) | async-done | bytes 1048608 | tf_op jit(solution)/shard_map/all_to_all | solution.py:24
  92.4 1.3 copy.48
  93.7 650.4 %all-reduce.3.cloned.1.call-done = (f32[2,512,512]{1,2,0:T(8,128)}, f32[2,512,512]{2,1,0:T(8,128)}, f32[2,512,512]{1,2,0:T(8,128)}) async-done(((f32[2,512,512]{1,2,0:T(8,128)}, f32[2,512,512]{2,1,0:T(8,128)}, f32[2,512,512]{1,2,0:T(8,128)}), (f32[2,512,512]{1,2,0:T(8,128)}, f32[2,512,512]{2,1,0:T(8,128)}, f32[2,512,512]{1,2,0:T(8,128)})) %all-reduce.3.cloned.1.call-update) | async-done | bytes 6291472 | tf_op jit(solution)/shard_map/psum | solution.py:57
  744.0 3.3 fusion
  748.6 1.4 convolution_bitcast_fusion.7
  750.0 1.4 convolution_bitcast_fusion.1
  753.8 1.3 multiply_convert_fusion
  755.2 3.1 convolution_convert_fusion.1
  758.3 3.1 convolution_convert_fusion
  761.4 2.3 copy_bitcast_fusion
  763.7 48.9 %all-to-all-start.4 = ((bf16[4,128,1024]{1,2,0:T(8,128)(2,1)}), bf16[4,128,1024]{1,2,0:T(8,128)(2,1)S(1)}, u32[]{:S(2)}, u32[]{:S(2)}) async-start(bf16[4,128,1024]{1,2,0:T(8,128)(2,1)} %copy_bitcast_fusion), calls=%async_computation.4 | async-start | bytes 2097152 | tf_op jit(solution)/shard_map/all_to_all | solution.py:71
  812.7 1.3 copy.57
  814.0 1.3 copy.56
  815.3 11.0 %all-to-all-done.4 = bf16[4,128,1024]{1,2,0:T(8,128)(2,1)S(1)} async-done(((bf16[4,128,1024]{1,2,0:T(8,128)(2,1)}), bf16[4,128,1024]{1,2,0:T(8,128)(2,1)S(1)}, u32[]{:S(2)}, u32[]{:S(2)}) %all-to-all-start.4) | async-done | bytes 1048608 | tf_op jit(solution)/shard_map/all_to_all | solution.py:71
  826.2 1.3 copy.55
  (57 shorter events, 17.3 us)
Async XLA Ops:
  8.4 9.4 %all-to-all-start = ((bf16[128,4,2]{0,2,1:T(2,128)(2,1)}), bf16[128,4,2]{0,2,1:T(2,128)(2,1)S(1)}, u32[]{:S(2)}, u32[]{:S(2)}) async-start(bf16[128,4,2]{0,2,1:T(2,128)(2,1)} %bitcast), calls=%async_computation | async-start | bytes 4096 | tf_op jit(solution)/shard_map/all_to_all | solution.py:27
  14.9 7.2 copy-start.10
  17.8 17.8 %all-to-all-start.2 = ((bf16[128,4,1024]{0,2,1:T(8,128)(2,1)}), bf16[128,4,1024]{0,2,1:T(8,128)(2,1)S(1)}, u32[]{:S(2)}, u32[]{:S(2)}) async-start(bf16[128,4,1024]{0,2,1:T(8,128)(2,1)} %bitcast.8), calls=%async_computation.2 | async-start | bytes 2097152 | tf_op jit(solution)/shard_map/all_to_all | solution.py:25
  35.6 18.0 %all-to-all-start.1 = ((bf16[128,4,1024]{0,2,1:T(8,128)(2,1)}), bf16[128,4,1024]{0,2,1:T(8,128)(2,1)S(1)}, u32[]{:S(2)}, u32[]{:S(2)}) async-start(bf16[128,4,1024]{0,2,1:T(8,128)(2,1)} %bitcast.4), calls=%async_computation.1 | async-start | bytes 2097152 | tf_op jit(solution)/shard_map/all_to_all | solution.py:26
  40.0 704.0 %all-reduce.3.cloned.1.call-start = ((), (), s32[]{:S(2)}) async-start(), calls=%async_computation.5 | async-start | bytes 12582912 | tf_op jit(solution)/shard_map/psum | solution.py:57
  40.5 2.6 copy-start.5
  40.5 4.0 copy-start.7
  46.0 8.9 %copy-start.3 = (bf16[2,512,512]{2,1,0:T(8,128)(2,1)S(1)}, bf16[2,512,512]{2,1,0:T(8,128)(2,1)}, u32[]{:S(2)}) copy-start(bf16[2,512,512]{2,1,0:T(8,128)(2,1)} %param.12) | copy-start | bytes 3145732
  54.9 1.6 copy-start.15
  56.5 1.2 copy-start.16
  57.7 1.2 copy-start.14
  59.6 1.2 copy-start.12
  60.8 1.2 copy-start.13
  68.0 1.2 copy-start.11
  69.3 5.7 copy-start.6
  70.6 21.8 %all-to-all-start.3 = ((bf16[128,4,1024]{0,2,1:T(8,128)(2,1)}), bf16[128,4,1024]{0,2,1:T(8,128)(2,1)S(1)}, u32[]{:S(2)}, u32[]{:S(2)}) async-start(bf16[128,4,1024]{0,2,1:T(8,128)(2,1)} %bitcast.23), calls=%async_computation.3 | async-start | bytes 2097152 | tf_op jit(solution)/shard_map/all_to_all | solution.py:24
  744.0 3.3 copy-start.1
  747.4 1.2 copy-start.8
  748.6 2.9 copy-start
  751.5 1.6 copy-start.2
  751.5 1.8 copy-start.4
  753.8 1.4 copy-start.9
  763.7 62.5 %all-to-all-start.4 = ((bf16[4,128,1024]{1,2,0:T(8,128)(2,1)}), bf16[4,128,1024]{1,2,0:T(8,128)(2,1)S(1)}, u32[]{:S(2)}, u32[]{:S(2)}) async-start(bf16[4,128,1024]{1,2,0:T(8,128)(2,1)} %copy_bitcast_fusion), calls=%async_computation.4 | async-start | bytes 2097152 | tf_op jit(solution)/shard_map/all_to_all | solution.py:71
Sparse Core Ops, SparseCore 0:
  68.2 675.7 all-reduce.2
where the time goes:
time: 835 us; the launch traced here: 834 us
  waiting for transfers between devices  696 us (83%)
  starting transfers between devices  68.3 us (8%)
  matrix products  21.9 us (3%)
  local copies, waits for them, and re-layouts  20.3 us (2%)
  between operations  14.2 us (2%)
  other arithmetic  13.9 us (2%)
    psum x1, waiting for transfers between devices, shards(): lax.psum((local_gate, local_down, local_up), 'tokens')  650 us
    all_to_all x1, starting transfers between devices, shards(): lax.all_to_all(grouped, 'heads', split_axis=0, concat_axis=1, tiled=True)  48.9 us
    unnamed x42, local copies, waits for them, and re-layouts  17.1 us
  transfers between devices with their start and end apart: 6, of which 6 were waited for; matrix products, arithmetic and copies ran while one was open for 2% of the time, Pallas kernels for 0%

commit v1 on v0

v1 whole, which is shorter than its diff:
```python
import functools

import jax
import jax.numpy as jnp
from jax import lax
from jax.experimental import pallas as pl
from jax.experimental.pallas import tpu as pltpu
from jax.sharding import PartitionSpec as P

MESH = pl.DeviceIdType.MESH
NX, NZ = 4, 8
ROWS = 128
WIDTH = 512
PAIR = 2 * WIDTH
MATS = 6
PIECE = WIDTH // (NX * NZ)

GROUPS = ((0, 2, "x"), (2, 1, "z"), (3, 3, "x"))


def dot(left, right, dims):
    return lax.dot_general(
        left, right, ((dims[:1], dims[1:]), ((), ())), preferred_element_type=jnp.float32
    )


def kernel(
    q_ref, k_ref, v_ref, rate_ref, gate_ref, down_ref, up_ref,
    out_ref, gate_out, down_out, up_out,
    d_own, k_all, d_all, q_all, hid, d_gate, d_up, grads, mixed, results, next_t,
    first_in, first_sum, second_in, second_sum, last_in,
    in_send, in_recv, red_send, red_recv, last_send, last_recv, gat_send, gat_recv,
    out_send, out_recv,
):
    group = lax.axis_index("heads")
    place = lax.axis_index("tokens")
    y_lo, core = group // 2, group % 2
    x, z, y_hi = place // 16, (place // 2) % 8, place % 2
    y = y_hi * 2 + y_lo

    def device(y, core, x, z):
        return ((y % 2) * 2 + core, (x * NZ + z) * 2 + y // 2)

    peers = {
        "x": [device(y, core, (x + step) % NX, z) for step in range(1, NX)],
        "z": [device(y, core, x, (z + step) % NZ) for step in range(1, NZ)],
    }
    position = {"x": x, "z": z}
    size = {"x": NX, "z": NZ}
    other = {"x": "z", "z": "x"}
    opposite = device((y + 2) % 4, core, x, z)
    sibling = device(y, 1 - core, x, z)
    forward = (y + 1 + 2 * core) % 4
    targets = [sibling, device(forward, 0, x, z), device(forward, 1, x, z)]
    below, above = device((y + 3) % 4, 0, x, z), device((y + 1) % 4, 1, x, z)
    sources = [sibling, below, above]
    target_group = [y_lo * 2 + 1 - core, (1 - y_lo) * 2, (1 - y_lo) * 2 + 1]
    target_slot = [1, 2 + core, 2 + core]
    source_group = [y_lo * 2 + 1 - core, (1 - y_lo) * 2, (1 - y_lo) * 2 + 1]

    barrier = pltpu.get_barrier_semaphore()
    greeted = peers["x"] + peers["z"] + [opposite] + targets + sources[1:]
    for peer in greeted:
        pl.semaphore_signal(barrier, inc=1, device_id=peer, device_id_type=MESH)

    for head in range(8):
        cols = slice(head * WIDTH, (head + 1) * WIDTH)
        d_own[:, cols] = (-rate_ref[:, head : head + 1] * v_ref[:, cols].astype(jnp.float32)).astype(
            jnp.bfloat16
        )
    pl.semaphore_wait(barrier, len(greeted))

    def columns(of_group, head):
        return pl.ds(pl.multiple_of(of_group * PAIR, PAIR) + head * WIDTH, WIDTH)

    def slot_rows(slot):
        if isinstance(slot, int):
            return pl.ds(slot * ROWS, ROWS)
        return pl.ds(pl.multiple_of(slot * ROWS, ROWS), ROWS)

    started = []

    def send(src, dst, send_sem, recv_sem, to):
        copy = pltpu.make_async_remote_copy(
            src_ref=src, dst_ref=dst, send_sem=send_sem, recv_sem=recv_sem,
            device_id=to, device_id_type=MESH,
        )
        copy.start()
        started.append(copy)
        return copy

    incoming = {}

    def exchange(which, src, dst, head):
        for n in (1, 2, 0):
            at = (which, head)
            if n == 0:
                recv_at = in_recv.at[which, head, 0]
            else:
                recv_at = in_recv.at[which, head, 1 + core]
            copy = send(
                src.at[:, columns(target_group[n], head)],
                dst.at[slot_rows(target_slot[n]), pl.ds(head * WIDTH, WIDTH)],
                in_send.at[which, head, n],
                recv_at,
                targets[n],
            )
        dst[slot_rows(0), pl.ds(head * WIDTH, WIDTH)] = src[:, columns(group, head)]

    def arrived(which, dst, head, n):
        there = dst.at[slot_rows(1 + n), pl.ds(head * WIDTH, WIDTH)]
        pltpu.make_async_remote_copy(
            src_ref=there, dst_ref=there, send_sem=in_send.at[which, head, n],
            recv_sem=in_recv.at[which, head, n], device_id=sources[n], device_id_type=MESH,
        ).wait_recv()

    for head in range(2):
        exchange(0, k_ref, k_all, head)
        exchange(1, d_own, d_all, head)

    def gradients(head):
        cols = slice(head * WIDTH, (head + 1) * WIDTH)
        for half in range(2):
            if half == 0:
                arrived(0, k_all, head, 0)
                arrived(1, d_all, head, 0)
            else:
                for n in (1, 2):
                    arrived(0, k_all, head, n)
                    arrived(1, d_all, head, n)
            rows = slice(half * 2 * ROWS, (half + 1) * 2 * ROWS)
            keys = k_all[rows, cols]
            d_out = d_all[rows, cols]
            gate_pre = dot(keys, gate_ref[head], (1, 0))
            up_pre = dot(keys, up_ref[head], (1, 0))
            d_hidden = dot(d_out, down_ref[head], (1, 1))
            sigma = jax.nn.sigmoid(gate_pre)
            silu = gate_pre * sigma
            hid[rows, :] = (silu * up_pre).astype(jnp.bfloat16)
            d_gate[rows, :] = (d_hidden * up_pre * sigma * (1.0 + gate_pre * (1.0 - sigma))).astype(
                jnp.bfloat16
            )
            d_up[rows, :] = (d_hidden * silu).astype(jnp.bfloat16)
        base = 3 * head
        grads[base] = dot(d_gate[...], k_all[:, cols], (0, 0)).astype(jnp.bfloat16)
        grads[base + 1] = dot(d_up[...], k_all[:, cols], (0, 0)).astype(jnp.bfloat16)
        grads[base + 2] = dot(d_all[:, cols], hid[...], (0, 0)).astype(jnp.bfloat16)

    def slab(axis, index, rows):
        return pl.ds(pl.multiple_of(index * rows, rows), rows)

    def reduce_start(g, level):
        first, count, axis = GROUPS[g]
        if level == 0:
            src, dst, rows = grads.at[first : first + count], first_in[g], WIDTH // size[axis]
        else:
            axis = other[axis]
            src, dst, rows = first_sum[g], second_in[g], PIECE
        for n, peer in enumerate(peers[axis]):
            index = (position[axis] + n + 1) % size[axis]
            incoming["reduce", g, level, n] = send(
                src.at[:, slab(axis, index, rows), :], dst.at[n],
                red_send.at[g, level, n], red_recv.at[g, level, n], peer,
            )

    def reduce_finish(g, level):
        first, count, axis = GROUPS[g]
        if level == 0:
            src, rows = grads.at[first : first + count], WIDTH // size[axis]
            dst, total = first_in[g], first_sum[g]
        else:
            axis = other[axis]
            src, rows = first_sum[g], PIECE
            dst, total = second_in[g], second_sum[g]
        for n in range(len(peers[axis])):
            incoming["reduce", g, level, n].wait_recv()
        for m in range(count):
            own = src[m, slab(axis, position[axis], rows), :].astype(jnp.float32)
            for n in range(len(peers[axis])):
                own = own + dst[n, m].astype(jnp.float32)
            total[m] = own.astype(jnp.bfloat16)

    def last_start(g):
        incoming["last", g] = send(
            second_sum[g], last_in[g], last_send.at[g], last_recv.at[g], opposite
        )

    def piece_start(g):
        axis = GROUPS[g][2]
        return position[axis] * (WIDTH // size[axis]) + position[other[axis]] * PIECE

    def renormed(g):
        first, count, axis = GROUPS[g]
        begin = piece_start(g)
        chosen = (
            lax.broadcasted_iota(jnp.int32, (PIECE, WIDTH), 1)
            == lax.broadcasted_iota(jnp.int32, (PIECE, WIDTH), 0) + begin
        )
        pick = jnp.where(chosen, 1.0, 0.0).astype(jnp.bfloat16)
        incoming["last", g].wait_recv()
        for m in range(count):
            head, kind = divmod(first + m, 3)
            weight = (gate_ref, up_ref, down_ref)[kind][head]
            wide = dot(pick, weight, (1, 1))
            total = second_sum[g][m].astype(jnp.float32) + last_in[g][m].astype(jnp.float32)
            moved = wide - total
            factor = jnp.sqrt(jnp.sum(wide * wide, axis=1, keepdims=True)) / jnp.sqrt(
                jnp.sum(moved * moved, axis=1, keepdims=True) + 1e-06
            )
            next_t[first + m, pl.ds(pl.multiple_of(begin, PIECE), PIECE), :] = (
                moved * factor
            ).astype(jnp.bfloat16)

    def gather_start(g, level):
        first, count, axis = GROUPS[g]
        if level == 0:
            axis = other[axis]
            begin, rows = piece_start(g), PIECE
        else:
            rows = WIDTH // size[axis]
            begin = position[axis] * rows
        here = next_t.at[first : first + count, pl.ds(pl.multiple_of(begin, rows), rows), :]
        for n, peer in enumerate(peers[axis]):
            incoming["gather", g, level, n] = send(
                here, here, gat_send.at[g, level, n], gat_recv.at[g, level, n], peer
            )

    def gather_finish(g, level):
        first, count, axis = GROUPS[g]
        if level == 0:
            axis = other[axis]
        for n in range(len(peers[axis])):
            incoming["gather", g, level, n].wait_recv()

    def of_head(head):
        return [g for g, (first, count, _) in enumerate(GROUPS) if first // 3 == head]

    for head in range(2):
        gradients(head)
        for g in of_head(head):
            reduce_start(g, 0)
        exchange(2, q_ref, q_all, head)
    everyone = range(len(GROUPS))
    for g in everyone:
        reduce_finish(g, 0)
        reduce_start(g, 1)
    for g in everyone:
        reduce_finish(g, 1)
        last_start(g)
    for g in everyone:
        renormed(g)
        gather_start(g, 0)
    for g in everyone:
        gather_finish(g, 0)
        gather_start(g, 1)

    for head in range(2):
        cols = slice(head * WIDTH, (head + 1) * WIDTH)
        for n in range(3):
            arrived(2, q_all, head, n)
        for g in of_head(head):
            gather_finish(g, 1)
        for half in (1, 0):
            rows = slice(half * 2 * ROWS, (half + 1) * 2 * ROWS)
            queries = q_all[rows, cols]
            first = dot(queries, next_t[3 * head], (1, 1))
            second = dot(queries, next_t[3 * head + 1], (1, 1))
            mixed[rows, :] = (first * jax.nn.sigmoid(first) * second).astype(jnp.bfloat16)
            results[rows, cols] = dot(mixed[rows, :], next_t[3 * head + 2], (1, 1)).astype(
                jnp.bfloat16
            )
            for n in ((1, 2) if half else (0,)):
                index = 0 if n == 0 else 1 + core
                send(
                    results.at[slot_rows(1 + n), cols], out_ref.at[:, columns(group, head)],
                    out_send.at[head, n], out_recv.at[head, index], sources[n],
                )
        out_ref[:, columns(group, head)] = results[slot_rows(0), cols]

    same = (
        lax.broadcasted_iota(jnp.int32, (WIDTH, WIDTH), 0)
        == lax.broadcasted_iota(jnp.int32, (WIDTH, WIDTH), 1)
    )
    unit = jnp.where(same, 1.0, 0.0).astype(jnp.bfloat16)
    for head in range(2):
        for kind, target in enumerate((gate_out, up_out, down_out)):
            target[head] = dot(unit, next_t[3 * head + kind], (1, 1)).astype(jnp.bfloat16)

    for head in range(2):
        for n in range(3):
            there = out_ref.at[:, columns(target_group[n], head)]
            pltpu.make_async_remote_copy(
                src_ref=there, dst_ref=there, send_sem=out_send.at[head, n],
                recv_sem=out_recv.at[head, n], device_id=targets[n], device_id_type=MESH,
            ).wait_recv()
    for copy in started:
        copy.wait_send()


def solution(mesh):
    def step(queries, keys, values, rates, gate_fast, down_fast, up_fast):
        size = {"x": NX, "z": NZ}
        bf16 = jnp.bfloat16

        def per_group(shape):
            return [pltpu.VMEM(shape(count, axis), bf16) for _, count, axis in GROUPS]

        slab = lambda axis: WIDTH // size[axis]
        rest = lambda axis: NX * NZ // size[axis]
        whole = pl.BlockSpec(memory_space=pltpu.VMEM)
        groups = len(GROUPS)
        return pl.pallas_call(
            kernel,
            out_shape=(
                jax.ShapeDtypeStruct(queries.shape, bf16),
                jax.ShapeDtypeStruct(gate_fast.shape, bf16),
                jax.ShapeDtypeStruct(down_fast.shape, bf16),
                jax.ShapeDtypeStruct(up_fast.shape, bf16),
            ),
            in_specs=[whole] * 7,
            out_specs=[whole] * 4,
            scratch_shapes=[
                pltpu.VMEM((ROWS, 8 * WIDTH), bf16),
                pltpu.VMEM((4 * ROWS, PAIR), bf16),
                pltpu.VMEM((4 * ROWS, PAIR), bf16),
                pltpu.VMEM((4 * ROWS, PAIR), bf16),
                pltpu.VMEM((4 * ROWS, WIDTH), bf16),
                pltpu.VMEM((4 * ROWS, WIDTH), bf16),
                pltpu.VMEM((4 * ROWS, WIDTH), bf16),
                pltpu.VMEM((MATS, WIDTH, WIDTH), bf16),
                pltpu.VMEM((4 * ROWS, WIDTH), bf16),
                pltpu.VMEM((4 * ROWS, PAIR), bf16),
                pltpu.VMEM((MATS, WIDTH, WIDTH), bf16),
                per_group(lambda count, axis: (size[axis] - 1, count, slab(axis), WIDTH)),
                per_group(lambda count, axis: (count, slab(axis), WIDTH)),
                per_group(lambda count, axis: (rest(axis) - 1, count, PIECE, WIDTH)),
                per_group(lambda count, axis: (count, PIECE, WIDTH)),
                per_group(lambda count, axis: (count, PIECE, WIDTH)),
                pltpu.SemaphoreType.DMA((3, 2, 3)),
                pltpu.SemaphoreType.DMA((3, 2, 3)),
                pltpu.SemaphoreType.DMA((groups, 2, NZ - 1)),
                pltpu.SemaphoreType.DMA((groups, 2, NZ - 1)),
                pltpu.SemaphoreType.DMA((groups,)),
                pltpu.SemaphoreType.DMA((groups,)),
                pltpu.SemaphoreType.DMA((groups, 2, NZ - 1)),
                pltpu.SemaphoreType.DMA((groups, 2, NZ - 1)),
                pltpu.SemaphoreType.DMA((2, 3)),
                pltpu.SemaphoreType.DMA((2, 3)),
            ],
            compiler_params=pltpu.CompilerParams(
                collective_id=0, has_side_effects=True, vmem_limit_bytes=56 << 20
            ),
        )(queries, keys, values, rates, gate_fast, down_fast, up_fast)

    tokens = P(("heads", "tokens"), None)
    weights = P("heads", None, None)
    return jax.shard_map(
        step,
        mesh=mesh,
        in_specs=(tokens,) * 4 + (weights,) * 3,
        out_specs=(tokens,) + (weights,) * 3,
        check_vma=False,
    )
```

time: 835 us -> 121 us (0.14)
  waiting for transfers between devices: 696 us -> 0 us
  Pallas kernels: 0 us -> 112 us
  starting transfers between devices: 68.3 us -> 0 us
  matrix products: 21.9 us -> 0 us
  other arithmetic: 13.9 us -> 0 us
  between operations: 14.2 us -> 0.65 us
  local copies, waits for them, and re-layouts: 20.3 us -> 7.97 us
    psum x1 -> x0, waiting for transfers between devices: 650 us -> none  [shards(): lax.psum((local_gate, local_down, local_up), 'tokens')]
    pallas_call x0 -> x1, Pallas kernels: none -> 112 us  [step(): pl.pallas_call(kernel, out_shape=(jax.ShapeDtypeStruct(queries.shape, bf1...]
    all_to_all x5 -> x0, starting transfers between devices: 68.3 us -> none  [the longest x1 48.9 us: shards(): lax.all_to_all(grouped, 'heads', split_axis=0, concat_axis=1, tiled=True)]
    all_to_all x5 -> x0, waiting for transfers between devices: 45.5 us -> none  [the longest x1 15.4 us: shards(): lax.all_to_all(queries, 'heads', split_axis=1, concat_axis=0, tiled=True)]
    dot_general x16 -> x0, matrix products: 21.9 us -> none  [the longest x2 6.2 us: shards(): jnp.dot(mixed, down_next[head], preferred_element_type=jnp.float32)]
    unnamed x42 -> x11, local copies, waits for them, and re-layouts: 17.1 us -> 7.97 us
  transfers between devices with their start and end apart: 6 -> 0, of which waited for: 6 -> 0; matrix products, arithmetic and copies ran while one was open for 2% -> 0% of each run, Pallas kernels for 0% -> 0%
where the time goes in v1:
time: 121 us
  Pallas kernels  112 us (93%)
  local copies, waits for them, and re-layouts  7.97 us (7%)
    pallas_call x1, Pallas kernels, step(): pl.pallas_call(kernel, out_shape=(jax.ShapeDtypeStruct(queries.shape, bf1...  112 us
    unnamed x11, local copies, waits for them, and re-layouts  7.97 us

profile of v1, /device:TPU:1, one launch (start us, length us, event | category | flops | bytes accessed | tf_op | source)
XLA Modules:
  0.0 121.0 jit_solution(13100278053553934955)
XLA Ops:
  0.6 1.4 %copy.11.rate_ref = f32[128,8]{1,0:T(8,128)} copy(f32[128,8]{0,1:T(8,128)} %param.10) | data formatting | bytes 8192 | tf_op args[3]
  2.0 112.4 %shard_map.102 = (bf16[128,4096]{1,0:T(8,128)(2,1)}, bf16[2,512,512]{2,1,0:T(8,128)(2,1)}, bf16[2,512,512]{2,1,0:T(8,128)(2,1)}, bf16[2,512,512]{2,1,0:T(8,128)(2,1)}) custom-call(bf16[128,4096]{1,0:T(8,128)(2,1)} %q_ref.1, bf16[128,4096]{1,0:T(8,128)(2,1)} %k_ref.1, bf16[128,4096]{1,0:T(8,128)(2,1)} %v_ref.1, f32[128,8]{1,0:T(8,128)} %copy.11.rate_ref, ...), custom_call_target="tpu_custom_call" | custom-call | tf_op jit(solution)/shard_map/pallas_call | solution.py:312
  114.4 0.0 copy-start.2
  114.4 2.4 %copy.16 = bf16[128,4096]{1,0:T(8,128)(2,1)} copy(bf16[128,4096]{1,0:T(8,128)(2,1)} %get-tuple-element.8) | data formatting | bytes 2097152
  116.8 0.0 copy-done.2
  116.8 0.0 copy-start.1
  116.8 1.0 copy.17
  117.8 0.6 copy-done.1
  118.4 0.0 copy-start
  118.4 1.0 copy.18
  119.4 0.6 copy-done
  120.0 1.0 copy.19
Async XLA Ops:
  114.4 2.4 %copy-start.2 = (bf16[2,512,512]{2,1,0:T(8,128)(2,1)S(1)}, bf16[2,512,512]{2,1,0:T(8,128)(2,1)}, u32[]{:S(2)}) copy-start(bf16[2,512,512]{2,1,0:T(8,128)(2,1)} %get-tuple-element.9) | copy-start | bytes 3145732
  116.8 1.6 %copy-start.1 = (bf16[2,512,512]{2,1,0:T(8,128)(2,1)S(1)}, bf16[2,512,512]{2,1,0:T(8,128)(2,1)}, u32[]{:S(2)}) copy-start(bf16[2,512,512]{2,1,0:T(8,128)(2,1)} %get-tuple-element.10) | copy-start | bytes 3145732
  118.4 1.6 %copy-start = (bf16[2,512,512]{2,1,0:T(8,128)(2,1)S(1)}, bf16[2,512,512]{2,1,0:T(8,128)(2,1)}, u32[]{:S(2)}) copy-start(bf16[2,512,512]{2,1,0:T(8,128)(2,1)} %get-tuple-element.11) | copy-start | bytes 3145732

commit v2 on v1

--- a/solution.py
+++ b/solution.py
@@ -15,7 +15,7 @@
 MATS = 6
 PIECE = WIDTH // (NX * NZ)
 
-GROUPS = ((0, 2, "x"), (2, 1, "z"), (3, 3, "x"))
+GROUPS = ((0, 2, "x"), (2, 1, "z"), (3, 2, "x"), (5, 1, "z"))
 
 
 def dot(left, right, dims):
@@ -25,12 +25,13 @@
 
 
 def kernel(
-    q_ref, k_ref, v_ref, rate_ref, gate_ref, down_ref, up_ref,
-    out_ref, gate_out, down_out, up_out,
-    d_own, k_all, d_all, q_all, hid, d_gate, d_up, grads, mixed, results, next_t,
+    q_hbm, k_hbm, v_hbm, rate_hbm, gate_hbm, down_hbm, up_hbm,
+    out_ref, next_t,
+    v_ref, rate_ref, gate_ref, down_ref, up_ref,
+    d_own, k_all, d_all, q_all, hid, d_gate, d_up, grads, mixed, results,
     first_in, first_sum, second_in, second_sum, last_in,
-    in_send, in_recv, red_send, red_recv, last_send, last_recv, gat_send, gat_recv,
-    out_send, out_recv,
+    local_sem, in_send, in_recv, red_send, red_recv, last_send, last_recv,
+    gat_send, gat_recv, for_send, for_recv, out_send, out_recv,
 ):
     group = lax.axis_index("heads")
     place = lax.axis_index("tokens")
@@ -63,13 +64,6 @@
     for peer in greeted:
         pl.semaphore_signal(barrier, inc=1, device_id=peer, device_id_type=MESH)
 
-    for head in range(8):
-        cols = slice(head * WIDTH, (head + 1) * WIDTH)
-        d_own[:, cols] = (-rate_ref[:, head : head + 1] * v_ref[:, cols].astype(jnp.float32)).astype(
-            jnp.bfloat16
-        )
-    pl.semaphore_wait(barrier, len(greeted))
-
     def columns(of_group, head):
         return pl.ds(pl.multiple_of(of_group * PAIR, PAIR) + head * WIDTH, WIDTH)
 
@@ -91,21 +85,46 @@
 
     incoming = {}
 
+    def local(src, dst, index):
+        copy = pltpu.make_async_copy(src, dst, local_sem.at[index])
+        copy.start()
+        return copy
+
+    own_cols = pl.ds(pl.multiple_of(group * PAIR, PAIR), PAIR)
+    loads = {
+        name: local(src, dst, index)
+        for index, (name, src, dst) in enumerate(
+            (
+                ("rate", rate_hbm, rate_ref),
+                ("value", v_hbm, v_ref),
+                ("key", k_hbm.at[:, own_cols], k_all.at[slot_rows(0), :]),
+                ("gate", gate_hbm, gate_ref),
+                ("up", up_hbm, up_ref),
+                ("down", down_hbm, down_ref),
+                ("query", q_hbm.at[:, own_cols], q_all.at[slot_rows(0), :]),
+            )
+        )
+    }
+
+    loads["rate"].wait()
+    rate_cols = jnp.transpose(rate_ref[...])
+    loads["value"].wait()
+    for head in range(8):
+        cols = slice(head * WIDTH, (head + 1) * WIDTH)
+        d_own[:, cols] = (-rate_cols[:, head : head + 1] * v_ref[:, cols].astype(jnp.float32)).astype(
+            jnp.bfloat16
+        )
+
+    pl.semaphore_wait(barrier, len(greeted))
+
     def exchange(which, src, dst, head):
         for n in (1, 2, 0):
-            at = (which, head)
-            if n == 0:
-                recv_at = in_recv.at[which, head, 0]
-            else:
-                recv_at = in_recv.at[which, head, 1 + core]
-            copy = send(
+            index = 0 if n == 0 else 1 + core
+            send(
                 src.at[:, columns(target_group[n], head)],
                 dst.at[slot_rows(target_slot[n]), pl.ds(head * WIDTH, WIDTH)],
-                in_send.at[which, head, n],
-                recv_at,
-                targets[n],
-            )
-        dst[slot_rows(0), pl.ds(head * WIDTH, WIDTH)] = src[:, columns(group, head)]
+                in_send.at[which, head, n], in_recv.at[which, head, index], targets[n],
+            )
 
     def arrived(which, dst, head, n):
         there = dst.at[slot_rows(1 + n), pl.ds(head * WIDTH, WIDTH)]
@@ -115,8 +134,11 @@
         ).wait_recv()
 
     for head in range(2):
-        exchange(0, k_ref, k_all, head)
+        exchange(0, k_hbm, k_all, head)
         exchange(1, d_own, d_all, head)
+    d_all[slot_rows(0), :] = d_own[:, own_cols]
+    for name in ("key", "gate", "up", "down"):
+        loads[name].wait()
 
     def gradients(head):
         cols = slice(head * WIDTH, (head + 1) * WIDTH)
@@ -142,9 +164,11 @@
             )
             d_up[rows, :] = (d_hidden * silu).astype(jnp.bfloat16)
         base = 3 * head
+        grads[base + 2] = dot(d_all[:, cols], hid[...], (0, 0)).astype(jnp.bfloat16)
+        reduce_start(2 * head + 1, 0)
         grads[base] = dot(d_gate[...], k_all[:, cols], (0, 0)).astype(jnp.bfloat16)
         grads[base + 1] = dot(d_up[...], k_all[:, cols], (0, 0)).astype(jnp.bfloat16)
-        grads[base + 2] = dot(d_all[:, cols], hid[...], (0, 0)).astype(jnp.bfloat16)
+        reduce_start(2 * head, 0)
 
     def slab(axis, index, rows):
         return pl.ds(pl.multiple_of(index * rows, rows), rows)
@@ -211,35 +235,51 @@
                 moved * factor
             ).astype(jnp.bfloat16)
 
-    def gather_start(g, level):
+    def piece(g, index):
         first, count, axis = GROUPS[g]
-        if level == 0:
-            axis = other[axis]
-            begin, rows = piece_start(g), PIECE
-        else:
-            rows = WIDTH // size[axis]
-            begin = position[axis] * rows
-        here = next_t.at[first : first + count, pl.ds(pl.multiple_of(begin, rows), rows), :]
+        begin = position[axis] * (WIDTH // size[axis]) + index * PIECE
+        return next_t.at[first : first + count, pl.ds(pl.multiple_of(begin, PIECE), PIECE), :]
+
+    def forward_piece(g, index):
+        for n, peer in enumerate(peers[GROUPS[g][2]]):
+            pltpu.make_async_remote_copy(
+                src_ref=piece(g, index), dst_ref=piece(g, index),
+                send_sem=for_send.at[g, n], recv_sem=for_recv.at[g, n],
+                device_id=peer, device_id_type=MESH,
+            ).start()
+
+    def gather_start(g):
+        axis = other[GROUPS[g][2]]
+        here = piece(g, position[axis])
         for n, peer in enumerate(peers[axis]):
-            incoming["gather", g, level, n] = send(
-                here, here, gat_send.at[g, level, n], gat_recv.at[g, level, n], peer
-            )
-
-    def gather_finish(g, level):
+            incoming["gather", g, n] = send(here, here, gat_send.at[g, n], gat_recv.at[g, n], peer)
+        forward_piece(g, position[axis])
+
+    def gather_forward(g):
+        axis = other[GROUPS[g][2]]
+        for n in range(len(peers[axis])):
+            incoming["gather", g, n].wait_recv()
+            forward_piece(g, (position[axis] + size[axis] - n - 1) % size[axis])
+
+    def whole_slab(g, n):
         first, count, axis = GROUPS[g]
-        if level == 0:
-            axis = other[axis]
-        for n in range(len(peers[axis])):
-            incoming["gather", g, level, n].wait_recv()
+        here = next_t.at[first : first + count, slab(axis, position[axis], WIDTH // size[axis]), :]
+        return pltpu.make_async_remote_copy(
+            src_ref=here, dst_ref=here, send_sem=for_send.at[g, n], recv_sem=for_recv.at[g, n],
+            device_id=peers[axis][n], device_id_type=MESH,
+        )
+
+    def gather_finish(g):
+        for n in range(len(peers[GROUPS[g][2]])):
+            whole_slab(g, n).wait_recv()
 
     def of_head(head):
         return [g for g, (first, count, _) in enumerate(GROUPS) if first // 3 == head]
 
     for head in range(2):
         gradients(head)
-        for g in of_head(head):
-            reduce_start(g, 0)
-        exchange(2, q_ref, q_all, head)
+    for head in range(2):
+        exchange(2, q_hbm, q_all, head)
     everyone = range(len(GROUPS))
     for g in everyone:
         reduce_finish(g, 0)
@@ -249,17 +289,17 @@
         last_start(g)
     for g in everyone:
         renormed(g)
-        gather_start(g, 0)
+        gather_start(g)
     for g in everyone:
-        gather_finish(g, 0)
-        gather_start(g, 1)
+        gather_forward(g)
+    loads["query"].wait()
 
     for head in range(2):
         cols = slice(head * WIDTH, (head + 1) * WIDTH)
         for n in range(3):
             arrived(2, q_all, head, n)
         for g in of_head(head):
-            gather_finish(g, 1)
+            gather_finish(g)
         for half in (1, 0):
             rows = slice(half * 2 * ROWS, (half + 1) * 2 * ROWS)
             queries = q_all[rows, cols]
@@ -276,15 +316,6 @@
                     out_send.at[head, n], out_recv.at[head, index], sources[n],
                 )
         out_ref[:, columns(group, head)] = results[slot_rows(0), cols]
-
-    same = (
-        lax.broadcasted_iota(jnp.int32, (WIDTH, WIDTH), 0)
-        == lax.broadcasted_iota(jnp.int32, (WIDTH, WIDTH), 1)
-    )
-    unit = jnp.where(same, 1.0, 0.0).astype(jnp.bfloat16)
-    for head in range(2):
-        for kind, target in enumerate((gate_out, up_out, down_out)):
-            target[head] = dot(unit, next_t[3 * head + kind], (1, 1)).astype(jnp.bfloat16)
 
     for head in range(2):
         for n in range(3):
@@ -295,6 +326,29 @@
             ).wait_recv()
     for copy in started:
         copy.wait_send()
+    for g in everyone:
+        for n in range(len(peers[GROUPS[g][2]])):
+            whole_slab(g, n).wait_send()
+
+
+def finish(staged, next_t, out_ref, gate_ref, down_ref, up_ref, turned, sems):
+    copies = [pltpu.make_async_copy(staged, out_ref, sems.at[MATS])]
+    copies[0].start()
+    same = (
+        lax.broadcasted_iota(jnp.int32, (WIDTH, WIDTH), 0)
+        == lax.broadcasted_iota(jnp.int32, (WIDTH, WIDTH), 1)
+    )
+    unit = jnp.where(same, 1.0, 0.0).astype(jnp.bfloat16)
+    for m in range(MATS):
+        head, kind = divmod(m, 3)
+        turned[m] = dot(unit, next_t[m], (1, 1)).astype(jnp.bfloat16)
+        copy = pltpu.make_async_copy(
+            turned.at[m], (gate_ref, up_ref, down_ref)[kind].at[head], sems.at[m]
+        )
+        copy.start()
+        copies.append(copy)
+    for copy in copies:
+        copy.wait()
 
 
 def solution(mesh):
@@ -307,19 +361,30 @@
 
         slab = lambda axis: WIDTH // size[axis]
         rest = lambda axis: NX * NZ // size[axis]
-        whole = pl.BlockSpec(memory_space=pltpu.VMEM)
+        vmem = pl.BlockSpec(memory_space=pltpu.VMEM)
+        anywhere = pl.BlockSpec(memory_space=pltpu.HBM)
         groups = len(GROUPS)
-        return pl.pallas_call(
+        weight = gate_fast.shape
+        outs = (
+            jax.ShapeDtypeStruct(queries.shape, bf16),
+            jax.ShapeDtypeStruct(weight, bf16),
+            jax.ShapeDtypeStruct(weight, bf16),
+            jax.ShapeDtypeStruct(weight, bf16),
+        )
+        staged, next_t = pl.pallas_call(
             kernel,
             out_shape=(
-                jax.ShapeDtypeStruct(queries.shape, bf16),
-                jax.ShapeDtypeStruct(gate_fast.shape, bf16),
-                jax.ShapeDtypeStruct(down_fast.shape, bf16),
-                jax.ShapeDtypeStruct(up_fast.shape, bf16),
+                pltpu.VMEM(queries.shape, bf16),
+                pltpu.VMEM((MATS, WIDTH, WIDTH), bf16),
             ),
-            in_specs=[whole] * 7,
-            out_specs=[whole] * 4,
+            in_specs=[anywhere] * 7,
+            out_specs=[vmem] * 2,
             scratch_shapes=[
+                pltpu.VMEM((ROWS, 8 * WIDTH), bf16),
+                pltpu.VMEM((8, ROWS), jnp.float32),
+                pltpu.VMEM(weight, bf16),
+                pltpu.VMEM(weight, bf16),
+                pltpu.VMEM(weight, bf16),
                 pltpu.VMEM((ROWS, 8 * WIDTH), bf16),
                 pltpu.VMEM((4 * ROWS, PAIR), bf16),
                 pltpu.VMEM((4 * ROWS, PAIR), bf16),
@@ -330,27 +395,45 @@
                 pltpu.VMEM((MATS, WIDTH, WIDTH), bf16),
                 pltpu.VMEM((4 * ROWS, WIDTH), bf16),
                 pltpu.VMEM((4 * ROWS, PAIR), bf16),
-                pltpu.VMEM((MATS, WIDTH, WIDTH), bf16),
                 per_group(lambda count, axis: (size[axis] - 1, count, slab(axis), WIDTH)),
                 per_group(lambda count, axis: (count, slab(axis), WIDTH)),
                 per_group(lambda count, axis: (rest(axis) - 1, count, PIECE, WIDTH)),
                 per_group(lambda count, axis: (count, PIECE, WIDTH)),
                 per_group(lambda count, axis: (count, PIECE, WIDTH)),
+                pltpu.SemaphoreType.DMA((7,)),
                 pltpu.SemaphoreType.DMA((3, 2, 3)),
                 pltpu.SemaphoreType.DMA((3, 2, 3)),
                 pltpu.SemaphoreType.DMA((groups, 2, NZ - 1)),
                 pltpu.SemaphoreType.DMA((groups, 2, NZ - 1)),
                 pltpu.SemaphoreType.DMA((groups,)),
                 pltpu.SemaphoreType.DMA((groups,)),
-                pltpu.SemaphoreType.DMA((groups, 2, NZ - 1)),
-                pltpu.SemaphoreType.DMA((groups, 2, NZ - 1)),
+                pltpu.SemaphoreType.DMA((groups, NZ - 1)),
+                pltpu.SemaphoreType.DMA((groups, NZ - 1)),
+                pltpu.SemaphoreType.DMA((groups, NZ - 1)),
+                pltpu.SemaphoreType.DMA((groups, NZ - 1)),
                 pltpu.SemaphoreType.DMA((2, 3)),
                 pltpu.SemaphoreType.DMA((2, 3)),
             ],
             compiler_params=pltpu.CompilerParams(
-                collective_id=0, has_side_effects=True, vmem_limit_bytes=56 << 20
+                collective_id=0, has_side_effects=True, vmem_limit_bytes=40 << 20
             ),
-        )(queries, keys, values, rates, gate_fast, down_fast, up_fast)
+        )(
+            *(
+                pltpu.with_memory_space_constraint(array, pltpu.HBM)
+                for array in (queries, keys, values, rates.T, gate_fast, down_fast, up_fast)
+            )
+        )
+        return pl.pallas_call(
+            finish,
+            out_shape=outs,
+            in_specs=[vmem] * 2,
+            out_specs=[anywhere] * 4,
+            scratch_shapes=[
+                pltpu.VMEM((MATS, WIDTH, WIDTH), bf16),
+                pltpu.SemaphoreType.DMA((MATS + 1,)),
+            ],
+            compiler_params=pltpu.CompilerParams(vmem_limit_bytes=12 << 20),
+        )(staged, next_t)
 
     tokens = P(("heads", "tokens"), None)
     weights = P("heads", None, None)

time: 121 us -> 103 us (0.85)
  Pallas kernels: 112 us -> 103 us
  local copies, waits for them, and re-layouts: 7.97 us -> 0 us
    pallas_call x1 -> x2, Pallas kernels: 112 us -> 103 us  [the longest x1 99.8 us: step(): pl.pallas_call(kernel, out_shape=(pltpu.VMEM(queries.shape, bf16), pltpu....]
    unnamed x11 -> x0, local copies, waits for them, and re-layouts: 7.97 us -> none
where the time goes in v2:
time: 103 us
  Pallas kernels  103 us (100%)
    pallas_call x1, Pallas kernels, step(): pl.pallas_call(kernel, out_shape=(pltpu.VMEM(queries.shape, bf16), pltpu....  99.8 us
    pallas_call x1, Pallas kernels, step(): pl.pallas_call(finish, out_shape=outs, in_specs=[vmem] * 2, out_specs=[an...  2.69 us

profile of v2, /device:TPU:1, one launch (start us, length us, event | category | flops | bytes accessed | tf_op | source)
XLA Modules:
  0.0 103.2 jit_solution(9452053797238272619)
XLA Ops:
  0.6 99.8 %shard_map.102 = (bf16[128,4096]{1,0:T(8,128)(2,1)S(1)}, bf16[6,512,512]{2,1,0:T(8,128)(2,1)S(1)}) custom-call(bf16[128,4096]{1,0:T(8,128)(2,1)} %q_hbm.1, bf16[128,4096]{1,0:T(8,128)(2,1)} %k_hbm.1, bf16[128,4096]{1,0:T(8,128)(2,1)} %v_hbm.1, f32[8,128]{1,0:T(8,128)} %bitcast.1, bf16[2,512,512]{2,1,0:T(8,128)(2,1)} %gate_hbm.1, ...), custom_call_target="tpu_custom_call" | custom-call | tf_op jit(solution)/shard_map/pallas_call | solution.py:374
  100.5 2.7 %shard_map.103 = (bf16[128,4096]{1,0:T(8,128)(2,1)}, bf16[2,512,512]{2,1,0:T(8,128)(2,1)}, bf16[2,512,512]{2,1,0:T(8,128)(2,1)}, bf16[2,512,512]{2,1,0:T(8,128)(2,1)}) custom-call(bf16[128,4096]{1,0:T(8,128)(2,1)S(1)} %get-tuple-element.6.staged, bf16[6,512,512]{2,1,0:T(8,128)(2,1)S(1)} %get-tuple-element.7.next_t), custom_call_target="tpu_custom_call" | custom-call | tf_op jit(solution)/shard_map/pallas_call | solution.py:426

commit v3 on v2

--- a/solution.py
+++ b/solution.py
@@ -15,7 +15,8 @@
 MATS = 6
 PIECE = WIDTH // (NX * NZ)
 
-GROUPS = ((0, 2, "x"), (2, 1, "z"), (3, 2, "x"), (5, 1, "z"))
+GROUPS = ((0, 2, "x", False), (2, 1, "z", False), (3, 2, "x", True), (5, 1, "x", False))
+PAIRED = 2
 
 
 def dot(left, right, dims):
@@ -32,6 +33,7 @@
     first_in, first_sum, second_in, second_sum, last_in,
     local_sem, in_send, in_recv, red_send, red_recv, last_send, last_recv,
     gat_send, gat_recv, for_send, for_recv, out_send, out_recv,
+    pair_in, pair_sum, pair_send, pair_recv,
 ):
     group = lax.axis_index("heads")
     place = lax.axis_index("tokens")
@@ -164,22 +166,47 @@
             )
             d_up[rows, :] = (d_hidden * silu).astype(jnp.bfloat16)
         base = 3 * head
-        grads[base + 2] = dot(d_all[:, cols], hid[...], (0, 0)).astype(jnp.bfloat16)
-        reduce_start(2 * head + 1, 0)
+        if head == 0:
+            grads[base + 2] = dot(d_all[:, cols], hid[...], (0, 0)).astype(jnp.bfloat16)
+            reduce_start(1, 0)
         grads[base] = dot(d_gate[...], k_all[:, cols], (0, 0)).astype(jnp.bfloat16)
         grads[base + 1] = dot(d_up[...], k_all[:, cols], (0, 0)).astype(jnp.bfloat16)
-        reduce_start(2 * head, 0)
+        if head == 0:
+            reduce_start(0, 0)
+        else:
+            pair_start()
+            grads[base + 2] = dot(d_all[:, cols], hid[...], (0, 0)).astype(jnp.bfloat16)
+            reduce_start(3, 0)
 
     def slab(axis, index, rows):
         return pl.ds(pl.multiple_of(index * rows, rows), rows)
 
+    def matrices(g):
+        first, count, _, paired = GROUPS[g]
+        return pl.ds(first + y_hi, 1) if paired else pl.ds(first, count)
+
+    def pair_start():
+        first = GROUPS[PAIRED][0]
+        incoming["pair"] = send(
+            grads.at[first + 1 - y_hi], pair_in, pair_send.at[0], pair_recv.at[0], opposite
+        )
+
+    def pair_finish():
+        first = GROUPS[PAIRED][0]
+        incoming["pair"].wait_recv()
+        pair_sum[0] = (
+            grads[first + y_hi].astype(jnp.float32) + pair_in[...].astype(jnp.float32)
+        ).astype(jnp.bfloat16)
+
+    def reduce_buffers(g, level):
+        _, count, axis, paired = GROUPS[g]
+        if level == 0:
+            src = pair_sum if paired else grads.at[matrices(g)]
+            return src, first_in[g], first_sum[g], axis, WIDTH // size[axis]
+        return first_sum[g], second_in[g], second_sum[g], other[axis], PIECE
+
     def reduce_start(g, level):
-        first, count, axis = GROUPS[g]
-        if level == 0:
-            src, dst, rows = grads.at[first : first + count], first_in[g], WIDTH // size[axis]
-        else:
-            axis = other[axis]
-            src, dst, rows = first_sum[g], second_in[g], PIECE
+        src, dst, _, axis, rows = reduce_buffers(g, level)
         for n, peer in enumerate(peers[axis]):
             index = (position[axis] + n + 1) % size[axis]
             incoming["reduce", g, level, n] = send(
@@ -188,17 +215,10 @@
             )
 
     def reduce_finish(g, level):
-        first, count, axis = GROUPS[g]
-        if level == 0:
-            src, rows = grads.at[first : first + count], WIDTH // size[axis]
-            dst, total = first_in[g], first_sum[g]
-        else:
-            axis = other[axis]
-            src, rows = first_sum[g], PIECE
-            dst, total = second_in[g], second_sum[g]
+        src, dst, total, axis, rows = reduce_buffers(g, level)
         for n in range(len(peers[axis])):
             incoming["reduce", g, level, n].wait_recv()
-        for m in range(count):
+        for m in range(total.shape[0]):
             own = src[m, slab(axis, position[axis], rows), :].astype(jnp.float32)
             for n in range(len(peers[axis])):
                 own = own + dst[n, m].astype(jnp.float32)
@@ -209,36 +229,41 @@
             second_sum[g], last_in[g], last_send.at[g], last_recv.at[g], opposite
         )
 
-    def piece_start(g):
-        axis = GROUPS[g][2]
-        return position[axis] * (WIDTH // size[axis]) + position[other[axis]] * PIECE
-
     def renormed(g):
-        first, count, axis = GROUPS[g]
-        begin = piece_start(g)
+        first, count, axis, paired = GROUPS[g]
+        begin = position[axis] * (WIDTH // size[axis]) + position[other[axis]] * PIECE
         chosen = (
             lax.broadcasted_iota(jnp.int32, (PIECE, WIDTH), 1)
             == lax.broadcasted_iota(jnp.int32, (PIECE, WIDTH), 0) + begin
         )
         pick = jnp.where(chosen, 1.0, 0.0).astype(jnp.bfloat16)
-        incoming["last", g].wait_recv()
-        for m in range(count):
-            head, kind = divmod(first + m, 3)
-            weight = (gate_ref, up_ref, down_ref)[kind][head]
-            wide = dot(pick, weight, (1, 1))
-            total = second_sum[g][m].astype(jnp.float32) + last_in[g][m].astype(jnp.float32)
+
+        def old(m):
+            head, kind = divmod(m, 3)
+            return dot(pick, (gate_ref, up_ref, down_ref)[kind][head], (1, 1))
+
+        if not paired:
+            incoming["last", g].wait_recv()
+        for m in range(1 if paired else count):
+            total = second_sum[g][m].astype(jnp.float32)
+            if paired:
+                wide = jnp.where(y_hi == 0, old(first), old(first + 1))
+            else:
+                wide = old(first + m)
+                total = total + last_in[g][m].astype(jnp.float32)
             moved = wide - total
             factor = jnp.sqrt(jnp.sum(wide * wide, axis=1, keepdims=True)) / jnp.sqrt(
                 jnp.sum(moved * moved, axis=1, keepdims=True) + 1e-06
             )
-            next_t[first + m, pl.ds(pl.multiple_of(begin, PIECE), PIECE), :] = (
-                moved * factor
-            ).astype(jnp.bfloat16)
+            index = first + y_hi if paired else first + m
+            next_t[index, pl.ds(pl.multiple_of(begin, PIECE), PIECE), :] = (moved * factor).astype(
+                jnp.bfloat16
+            )
 
     def piece(g, index):
-        first, count, axis = GROUPS[g]
+        axis = GROUPS[g][2]
         begin = position[axis] * (WIDTH // size[axis]) + index * PIECE
-        return next_t.at[first : first + count, pl.ds(pl.multiple_of(begin, PIECE), PIECE), :]
+        return next_t.at[matrices(g), pl.ds(pl.multiple_of(begin, PIECE), PIECE), :]
 
     def forward_piece(g, index):
         for n, peer in enumerate(peers[GROUPS[g][2]]):
@@ -262,8 +287,8 @@
             forward_piece(g, (position[axis] + size[axis] - n - 1) % size[axis])
 
     def whole_slab(g, n):
-        first, count, axis = GROUPS[g]
-        here = next_t.at[first : first + count, slab(axis, position[axis], WIDTH // size[axis]), :]
+        axis = GROUPS[g][2]
+        here = next_t.at[matrices(g), slab(axis, position[axis], WIDTH // size[axis]), :]
         return pltpu.make_async_remote_copy(
             src_ref=here, dst_ref=here, send_sem=for_send.at[g, n], recv_sem=for_recv.at[g, n],
             device_id=peers[axis][n], device_id_type=MESH,
@@ -273,33 +298,64 @@
         for n in range(len(peers[GROUPS[g][2]])):
             whole_slab(g, n).wait_recv()
 
-    def of_head(head):
-        return [g for g, (first, count, _) in enumerate(GROUPS) if first // 3 == head]
+    def share_slab(index):
+        here = next_t.at[matrices(PAIRED), slab("x", index, WIDTH // NX), :]
+        pltpu.make_async_remote_copy(
+            src_ref=here, dst_ref=here, send_sem=pair_send.at[1], recv_sem=pair_recv.at[1],
+            device_id=opposite, device_id_type=MESH,
+        ).start()
+
+    def share():
+        share_slab(x)
+        for n in range(NX - 1):
+            whole_slab(PAIRED, n).wait_recv()
+            share_slab((x + NX - n - 1) % NX)
+
+    def shared():
+        here = next_t.at[matrices(PAIRED)]
+        return pltpu.make_async_remote_copy(
+            src_ref=here, dst_ref=here, send_sem=pair_send.at[1], recv_sem=pair_recv.at[1],
+            device_id=opposite, device_id_type=MESH,
+        )
 
     for head in range(2):
         gradients(head)
     for head in range(2):
         exchange(2, q_hbm, q_all, head)
-    everyone = range(len(GROUPS))
-    for g in everyone:
-        reduce_finish(g, 0)
-        reduce_start(g, 1)
-    for g in everyone:
-        reduce_finish(g, 1)
-        last_start(g)
-    for g in everyone:
+    for g in (0, 1, 2, 3):
+        if g == PAIRED:
+            pair_finish()
+        else:
+            reduce_finish(g, 0)
+        reduce_start(g, 0 if g == PAIRED else 1)
+    for g in (0, 1, 2, 3):
+        if g == PAIRED:
+            reduce_finish(g, 0)
+            reduce_start(g, 1)
+        else:
+            reduce_finish(g, 1)
+            last_start(g)
+    for g in (0, 1, 3):
         renormed(g)
         gather_start(g)
-    for g in everyone:
+    reduce_finish(PAIRED, 1)
+    renormed(PAIRED)
+    gather_start(PAIRED)
+    for g in (0, 1, 3, 2):
         gather_forward(g)
+    share()
     loads["query"].wait()
 
     for head in range(2):
         cols = slice(head * WIDTH, (head + 1) * WIDTH)
         for n in range(3):
             arrived(2, q_all, head, n)
-        for g in of_head(head):
-            gather_finish(g)
+        if head == 0:
+            gather_finish(0)
+            gather_finish(1)
+        else:
+            gather_finish(3)
+            shared().wait_recv()
         for half in (1, 0):
             rows = slice(half * 2 * ROWS, (half + 1) * 2 * ROWS)
             queries = q_all[rows, cols]
@@ -326,7 +382,8 @@
             ).wait_recv()
     for copy in started:
         copy.wait_send()
-    for g in everyone:
+    shared().wait_send()
+    for g in range(len(GROUPS)):
         for n in range(len(peers[GROUPS[g][2]])):
             whole_slab(g, n).wait_send()
 
@@ -357,7 +414,10 @@
         bf16 = jnp.bfloat16
 
         def per_group(shape):
-            return [pltpu.VMEM(shape(count, axis), bf16) for _, count, axis in GROUPS]
+            return [
+                pltpu.VMEM(shape(1 if paired else count, axis), bf16)
+                for _, count, axis, paired in GROUPS
+            ]
 
         slab = lambda axis: WIDTH // size[axis]
         rest = lambda axis: NX * NZ // size[axis]
@@ -413,6 +473,10 @@
                 pltpu.SemaphoreType.DMA((groups, NZ - 1)),
                 pltpu.SemaphoreType.DMA((2, 3)),
                 pltpu.SemaphoreType.DMA((2, 3)),
+                pltpu.VMEM((WIDTH, WIDTH), bf16),
+                pltpu.VMEM((1, WIDTH, WIDTH), bf16),
+                pltpu.SemaphoreType.DMA((2,)),
+                pltpu.SemaphoreType.DMA((2,)),
             ],
             compiler_params=pltpu.CompilerParams(
                 collective_id=0, has_side_effects=True, vmem_limit_bytes=40 << 20

time: 103 us -> 97.5 us (0.947)
  Pallas kernels: 103 us -> 96.4 us
    pallas_call x1, Pallas kernels: 99.8 us -> 93.7 us  [step(): pl.pallas_call(kernel, out_shape=(pltpu.VMEM(queries.shape, bf16), pltpu....]
where the time goes in v3:
time: 97.5 us; the launch traced here: 97 us
  Pallas kernels  96.4 us (99%)
    pallas_call x1, Pallas kernels, step(): pl.pallas_call(kernel, out_shape=(pltpu.VMEM(queries.shape, bf16), pltpu....  93.7 us
    pallas_call x1, Pallas kernels, step(): pl.pallas_call(finish, out_shape=outs, in_specs=[vmem] * 2, out_specs=[an...  2.69 us

profile of v3, /device:TPU:1, one launch (start us, length us, event | category | flops | bytes accessed | tf_op | source)
XLA Modules:
  0.0 97.0 jit_solution(12602080628492278326)
XLA Ops:
  0.6 93.7 %shard_map.102 = (bf16[128,4096]{1,0:T(8,128)(2,1)S(1)}, bf16[6,512,512]{2,1,0:T(8,128)(2,1)S(1)}) custom-call(bf16[128,4096]{1,0:T(8,128)(2,1)} %q_hbm.1, bf16[128,4096]{1,0:T(8,128)(2,1)} %k_hbm.1, bf16[128,4096]{1,0:T(8,128)(2,1)} %v_hbm.1, f32[8,128]{1,0:T(8,128)} %bitcast.1, bf16[2,512,512]{2,1,0:T(8,128)(2,1)} %gate_hbm.1, ...), custom_call_target="tpu_custom_call" | custom-call | tf_op jit(solution)/shard_map/pallas_call | solution.py:434
  94.4 2.7 %shard_map.103 = (bf16[128,4096]{1,0:T(8,128)(2,1)}, bf16[2,512,512]{2,1,0:T(8,128)(2,1)}, bf16[2,512,512]{2,1,0:T(8,128)(2,1)}, bf16[2,512,512]{2,1,0:T(8,128)(2,1)}) custom-call(bf16[128,4096]{1,0:T(8,128)(2,1)S(1)} %get-tuple-element.6.staged, bf16[6,512,512]{2,1,0:T(8,128)(2,1)S(1)} %get-tuple-element.7.next_t), custom_call_target="tpu_custom_call" | custom-call | tf_op jit(solution)/shard_map/pallas_call | solution.py:490

commit v4 on v3

--- a/solution.py
+++ b/solution.py
@@ -17,6 +17,8 @@
 
 GROUPS = ((0, 2, "x", False), (2, 1, "z", False), (3, 2, "x", True), (5, 1, "x", False))
 PAIRED = 2
+CHUNKS = (1, 1, 2, 2)
+FAR = {1: (0,), 2: (1, 0), 4: (2, 1, 3, 0), 8: (4, 3, 5, 2, 6, 1, 7, 0)}
 
 
 def dot(left, right, dims):
@@ -27,11 +29,11 @@
 
 def kernel(
     q_hbm, k_hbm, v_hbm, rate_hbm, gate_hbm, down_hbm, up_hbm,
-    out_ref, next_t,
+    out_ref, turned,
     v_ref, rate_ref, gate_ref, down_ref, up_ref,
-    d_own, k_all, d_all, q_all, hid, d_gate, d_up, grads, mixed, results,
+    d_own, k_all, d_all, q_all, hid, d_gate, d_up, grads, mixed, results, next_t,
     first_in, first_sum, second_in, second_sum, last_in,
-    local_sem, in_send, in_recv, red_send, red_recv, last_send, last_recv,
+    local_sem, in_send, in_recv, slab_send, slab_recv, red_send, red_recv, last_send, last_recv,
     gat_send, gat_recv, for_send, for_recv, out_send, out_recv,
     pair_in, pair_sum, pair_send, pair_recv,
 ):
@@ -168,15 +170,15 @@
         base = 3 * head
         if head == 0:
             grads[base + 2] = dot(d_all[:, cols], hid[...], (0, 0)).astype(jnp.bfloat16)
-            reduce_start(1, 0)
+            reduce_start(1)
         grads[base] = dot(d_gate[...], k_all[:, cols], (0, 0)).astype(jnp.bfloat16)
         grads[base + 1] = dot(d_up[...], k_all[:, cols], (0, 0)).astype(jnp.bfloat16)
         if head == 0:
-            reduce_start(0, 0)
+            reduce_start(0)
         else:
             pair_start()
             grads[base + 2] = dot(d_all[:, cols], hid[...], (0, 0)).astype(jnp.bfloat16)
-            reduce_start(3, 0)
+            reduce_start(3)
 
     def slab(axis, index, rows):
         return pl.ds(pl.multiple_of(index * rows, rows), rows)
@@ -185,44 +187,111 @@
         first, count, _, paired = GROUPS[g]
         return pl.ds(first + y_hi, 1) if paired else pl.ds(first, count)
 
+    def at_rows(start, rows):
+        return pl.ds(pl.multiple_of(start, PIECE), rows)
+
+    def chunk(g, k):
+        axis = GROUPS[g][2]
+        far, chunks = other[axis], CHUNKS[g]
+        owners = size[far] // chunks
+        index = (position[far] // owners + k) % chunks
+        return index * owners * PIECE, owners * PIECE, index * owners
+
+    def pair_copy(k, part):
+        start, rows, _ = chunk(PAIRED, k)
+        here = at_rows(part * (WIDTH // NX) + start, rows)
+        return pltpu.make_async_remote_copy(
+            src_ref=grads.at[GROUPS[PAIRED][0] + 1 - y_hi, here, :], dst_ref=pair_in.at[here, :],
+            send_sem=pair_send.at[0], recv_sem=pair_recv.at[1 + k],
+            device_id=opposite, device_id_type=MESH,
+        )
+
     def pair_start():
-        first = GROUPS[PAIRED][0]
-        incoming["pair"] = send(
-            grads.at[first + 1 - y_hi], pair_in, pair_send.at[0], pair_recv.at[0], opposite
-        )
-
-    def pair_finish():
-        first = GROUPS[PAIRED][0]
-        incoming["pair"].wait_recv()
-        pair_sum[0] = (
-            grads[first + y_hi].astype(jnp.float32) + pair_in[...].astype(jnp.float32)
-        ).astype(jnp.bfloat16)
-
-    def reduce_buffers(g, level):
-        _, count, axis, paired = GROUPS[g]
-        if level == 0:
-            src = pair_sum if paired else grads.at[matrices(g)]
-            return src, first_in[g], first_sum[g], axis, WIDTH // size[axis]
-        return first_sum[g], second_in[g], second_sum[g], other[axis], PIECE
-
-    def reduce_start(g, level):
-        src, dst, _, axis, rows = reduce_buffers(g, level)
-        for n, peer in enumerate(peers[axis]):
-            index = (position[axis] + n + 1) % size[axis]
-            incoming["reduce", g, level, n] = send(
-                src.at[:, slab(axis, index, rows), :], dst.at[n],
-                red_send.at[g, level, n], red_recv.at[g, level, n], peer,
-            )
-
-    def reduce_finish(g, level):
-        src, dst, total, axis, rows = reduce_buffers(g, level)
+        for k in FAR[CHUNKS[PAIRED]]:
+            for part in range(NX):
+                pair_copy(k, part).start()
+
+    def pair_chunk(k):
+        start, rows, _ = chunk(PAIRED, k)
+        four = pair_in.at[pl.ds(0, NX * rows), :]
+        pltpu.make_async_remote_copy(
+            src_ref=four, dst_ref=four, send_sem=pair_send.at[0], recv_sem=pair_recv.at[1 + k],
+            device_id=opposite, device_id_type=MESH,
+        ).wait_recv()
+        for part in range(NX):
+            here = at_rows(part * (WIDTH // NX) + start, rows)
+            pair_sum[0, here, :] = (
+                grads[GROUPS[PAIRED][0] + y_hi, here, :].astype(jnp.float32)
+                + pair_in[here, :].astype(jnp.float32)
+            ).astype(jnp.bfloat16)
+        reduce_chunk_start(PAIRED, k)
+
+    def slab_copy(g, k, n):
+        axis = GROUPS[g][2]
+        start, rows, _ = chunk(g, k)
+        src = pair_sum if GROUPS[g][3] else grads.at[matrices(g)]
+        target = (position[axis] + n + 1) % size[axis]
+        return pltpu.make_async_remote_copy(
+            src_ref=src.at[:, at_rows(target * (WIDTH // size[axis]) + start, rows), :],
+            dst_ref=first_in[g].at[n, :, at_rows(start, rows), :],
+            send_sem=slab_send.at[g, n], recv_sem=slab_recv.at[g, k, n],
+            device_id=peers[axis][n], device_id_type=MESH,
+        )
+
+    def reduce_chunk_start(g, k):
+        for n in range(len(peers[GROUPS[g][2]])):
+            slab_copy(g, k, n).start()
+
+    def reduce_start(g):
+        for k in FAR[CHUNKS[g]]:
+            reduce_chunk_start(g, k)
+
+    def owner(axis, index):
+        return device(y, core, index, z) if axis == "x" else device(y, core, x, index)
+
+    def reduce_chunk(g, k):
+        axis = GROUPS[g][2]
+        far = other[axis]
+        start, rows, begin = chunk(g, k)
+        src = pair_sum if GROUPS[g][3] else grads.at[matrices(g)]
         for n in range(len(peers[axis])):
-            incoming["reduce", g, level, n].wait_recv()
-        for m in range(total.shape[0]):
-            own = src[m, slab(axis, position[axis], rows), :].astype(jnp.float32)
+            slab_copy(g, k, n).wait_recv()
+        here = at_rows(start, rows)
+        mine = at_rows(position[axis] * (WIDTH // size[axis]) + start, rows)
+        for m in range(first_sum[g].shape[0]):
+            own = src[m, mine, :].astype(jnp.float32)
             for n in range(len(peers[axis])):
-                own = own + dst[n, m].astype(jnp.float32)
-            total[m] = own.astype(jnp.bfloat16)
+                own = own + first_in[g][n, m, here, :].astype(jnp.float32)
+            first_sum[g][m, here, :] = own.astype(jnp.bfloat16)
+        owners = size[far] // CHUNKS[g]
+        for d in range(owners):
+            if k == 0 and d == 0:
+                continue
+            index = begin + (position[far] + d) % owners
+            slot = k * owners + d - 1
+            incoming["reduce", g, slot] = send(
+                first_sum[g].at[:, at_rows(index * PIECE, PIECE), :], second_in[g].at[slot],
+                red_send.at[g, slot], red_recv.at[g, slot], owner(far, index),
+            )
+
+    def reduce_sent(g):
+        axis = GROUPS[g][2]
+        for n in range(len(peers[axis])):
+            slab = first_in[g].at[n]
+            pltpu.make_async_remote_copy(
+                src_ref=slab, dst_ref=slab, send_sem=slab_send.at[g, n],
+                recv_sem=slab_recv.at[g, 0, n], device_id=peers[axis][n], device_id_type=MESH,
+            ).wait_send()
+
+    def reduce_finish(g):
+        far = other[GROUPS[g][2]]
+        for n in range(len(peers[far])):
+            incoming["reduce", g, n].wait_recv()
+        for m in range(second_sum[g].shape[0]):
+            own = first_sum[g][m, at_rows(position[far] * PIECE, PIECE), :].astype(jnp.float32)
+            for n in range(len(peers[far])):
+                own = own + second_in[g][n, m].astype(jnp.float32)
+            second_sum[g][m] = own.astype(jnp.bfloat16)
 
     def last_start(g):
         incoming["last", g] = send(
@@ -301,7 +370,7 @@
     def share_slab(index):
         here = next_t.at[matrices(PAIRED), slab("x", index, WIDTH // NX), :]
         pltpu.make_async_remote_copy(
-            src_ref=here, dst_ref=here, send_sem=pair_send.at[1], recv_sem=pair_recv.at[1],
+            src_ref=here, dst_ref=here, send_sem=pair_send.at[1], recv_sem=pair_recv.at[0],
             device_id=opposite, device_id_type=MESH,
         ).start()
 
@@ -314,7 +383,7 @@
     def shared():
         here = next_t.at[matrices(PAIRED)]
         return pltpu.make_async_remote_copy(
-            src_ref=here, dst_ref=here, send_sem=pair_send.at[1], recv_sem=pair_recv.at[1],
+            src_ref=here, dst_ref=here, send_sem=pair_send.at[1], recv_sem=pair_recv.at[0],
             device_id=opposite, device_id_type=MESH,
         )
 
@@ -322,30 +391,36 @@
         gradients(head)
     for head in range(2):
         exchange(2, q_hbm, q_all, head)
-    for g in (0, 1, 2, 3):
-        if g == PAIRED:
-            pair_finish()
-        else:
-            reduce_finish(g, 0)
-        reduce_start(g, 0 if g == PAIRED else 1)
-    for g in (0, 1, 2, 3):
-        if g == PAIRED:
-            reduce_finish(g, 0)
-            reduce_start(g, 1)
-        else:
-            reduce_finish(g, 1)
-            last_start(g)
+    for g in (0, 1):
+        for k in FAR[CHUNKS[g]]:
+            reduce_chunk(g, k)
+    order = FAR[CHUNKS[PAIRED]]
+    for k in order:
+        pair_chunk(k)
+        reduce_chunk(3, k)
+    for g in (0, 1):
+        reduce_finish(g)
+        last_start(g)
+    for k in order:
+        reduce_chunk(PAIRED, k)
+    reduce_finish(3)
+    last_start(3)
     for g in (0, 1, 3):
         renormed(g)
         gather_start(g)
-    reduce_finish(PAIRED, 1)
+    reduce_finish(PAIRED)
     renormed(PAIRED)
     gather_start(PAIRED)
-    for g in (0, 1, 3, 2):
+    for g in (0, 1, 3, PAIRED):
         gather_forward(g)
     share()
     loads["query"].wait()
 
+    same = (
+        lax.broadcasted_iota(jnp.int32, (WIDTH, WIDTH), 0)
+        == lax.broadcasted_iota(jnp.int32, (WIDTH, WIDTH), 1)
+    )
+    unit = jnp.where(same, 1.0, 0.0).astype(jnp.bfloat16)
     for head in range(2):
         cols = slice(head * WIDTH, (head + 1) * WIDTH)
         for n in range(3):
@@ -372,6 +447,8 @@
                     out_send.at[head, n], out_recv.at[head, index], sources[n],
                 )
         out_ref[:, columns(group, head)] = results[slot_rows(0), cols]
+    for m in range(MATS):
+        turned[m] = dot(unit, next_t[m], (1, 1)).astype(jnp.bfloat16)
 
     for head in range(2):
         for n in range(3):
@@ -383,27 +460,27 @@
     for copy in started:
         copy.wait_send()
     shared().wait_send()
+    pltpu.make_async_remote_copy(
+        src_ref=pair_in, dst_ref=pair_in, send_sem=pair_send.at[0], recv_sem=pair_recv.at[0],
+        device_id=opposite, device_id_type=MESH,
+    ).wait_send()
     for g in range(len(GROUPS)):
+        reduce_sent(g)
         for n in range(len(peers[GROUPS[g][2]])):
             whole_slab(g, n).wait_send()
 
 
-def finish(staged, next_t, out_ref, gate_ref, down_ref, up_ref, turned, sems):
+def finish(staged, turned, out_ref, gate_ref, down_ref, up_ref, sems):
     copies = [pltpu.make_async_copy(staged, out_ref, sems.at[MATS])]
-    copies[0].start()
-    same = (
-        lax.broadcasted_iota(jnp.int32, (WIDTH, WIDTH), 0)
-        == lax.broadcasted_iota(jnp.int32, (WIDTH, WIDTH), 1)
-    )
-    unit = jnp.where(same, 1.0, 0.0).astype(jnp.bfloat16)
     for m in range(MATS):
         head, kind = divmod(m, 3)
-        turned[m] = dot(unit, next_t[m], (1, 1)).astype(jnp.bfloat16)
-        copy = pltpu.make_async_copy(
-            turned.at[m], (gate_ref, up_ref, down_ref)[kind].at[head], sems.at[m]
-        )
+        copies.append(
+            pltpu.make_async_copy(
+                turned.at[m], (gate_ref, up_ref, down_ref)[kind].at[head], sems.at[m]
+            )
+        )
+    for copy in copies:
         copy.start()
-        copies.append(copy)
     for copy in copies:
         copy.wait()
 
@@ -431,7 +508,7 @@
             jax.ShapeDtypeStruct(weight, bf16),
             jax.ShapeDtypeStruct(weight, bf16),
         )
-        staged, next_t = pl.pallas_call(
+        staged, turned = pl.pallas_call(
             kernel,
             out_shape=(
                 pltpu.VMEM(queries.shape, bf16),
@@ -455,6 +532,7 @@
                 pltpu.VMEM((MATS, WIDTH, WIDTH), bf16),
                 pltpu.VMEM((4 * ROWS, WIDTH), bf16),
                 pltpu.VMEM((4 * ROWS, PAIR), bf16),
+                pltpu.VMEM((MATS, WIDTH, WIDTH), bf16),
                 per_group(lambda count, axis: (size[axis] - 1, count, slab(axis), WIDTH)),
                 per_group(lambda count, axis: (count, slab(axis), WIDTH)),
                 per_group(lambda count, axis: (rest(axis) - 1, count, PIECE, WIDTH)),
@@ -463,8 +541,10 @@
                 pltpu.SemaphoreType.DMA((7,)),
                 pltpu.SemaphoreType.DMA((3, 2, 3)),
                 pltpu.SemaphoreType.DMA((3, 2, 3)),
-                pltpu.SemaphoreType.DMA((groups, 2, NZ - 1)),
-                pltpu.SemaphoreType.DMA((groups, 2, NZ - 1)),
+                pltpu.SemaphoreType.DMA((groups, NZ - 1)),
+                pltpu.SemaphoreType.DMA((groups, NZ, NZ - 1)),
+                pltpu.SemaphoreType.DMA((groups, NZ - 1)),
+                pltpu.SemaphoreType.DMA((groups, NZ - 1)),
                 pltpu.SemaphoreType.DMA((groups,)),
                 pltpu.SemaphoreType.DMA((groups,)),
                 pltpu.SemaphoreType.DMA((groups, NZ - 1)),
@@ -476,7 +556,7 @@
                 pltpu.VMEM((WIDTH, WIDTH), bf16),
                 pltpu.VMEM((1, WIDTH, WIDTH), bf16),
                 pltpu.SemaphoreType.DMA((2,)),
-                pltpu.SemaphoreType.DMA((2,)),
+                pltpu.SemaphoreType.DMA((1 + NZ,)),
             ],
             compiler_params=pltpu.CompilerParams(
                 collective_id=0, has_side_effects=True, vmem_limit_bytes=40 << 20
@@ -492,12 +572,9 @@
             out_shape=outs,
             in_specs=[vmem] * 2,
             out_specs=[anywhere] * 4,
-            scratch_shapes=[
-                pltpu.VMEM((MATS, WIDTH, WIDTH), bf16),
-                pltpu.SemaphoreType.DMA((MATS + 1,)),
-            ],
+            scratch_shapes=[pltpu.SemaphoreType.DMA((MATS + 1,))],
             compiler_params=pltpu.CompilerParams(vmem_limit_bytes=12 << 20),
-        )(staged, next_t)
+        )(staged, turned)
 
     tokens = P(("heads", "tokens"), None)
     weights = P("heads", None, None)

time: 97.5 us -> 98.9 us (1.014)
  Pallas kernels: 96.4 us -> 98.1 us
    pallas_call x1, Pallas kernels: 93.7 us -> 96.1 us  [step(): pl.pallas_call(kernel, out_shape=(pltpu.VMEM(queries.shape, bf16), pltpu....]
where the time goes in v4:
time: 98.9 us; the launch traced here: 98.8 us
  Pallas kernels  98.1 us (99%)
    pallas_call x1, Pallas kernels, step(): pl.pallas_call(kernel, out_shape=(pltpu.VMEM(queries.shape, bf16), pltpu....  96.1 us
    pallas_call x1, Pallas kernels, step(): pl.pallas_call(finish, out_shape=outs, in_specs=[vmem] * 2, out_specs=[an...  2.06 us

profile of v4, /device:TPU:1, one launch (start us, length us, event | category | flops | bytes accessed | tf_op | source)
XLA Modules:
  0.0 98.8 jit_solution(16896347953905657887)
XLA Ops:
  0.6 96.1 %shard_map.102 = (bf16[128,4096]{1,0:T(8,128)(2,1)S(1)}, bf16[6,512,512]{2,1,0:T(8,128)(2,1)S(1)}) custom-call(bf16[128,4096]{1,0:T(8,128)(2,1)} %q_hbm.1, bf16[128,4096]{1,0:T(8,128)(2,1)} %k_hbm.1, bf16[128,4096]{1,0:T(8,128)(2,1)} %v_hbm.1, f32[8,128]{1,0:T(8,128)} %bitcast.1, bf16[2,512,512]{2,1,0:T(8,128)(2,1)} %gate_hbm.1, ...), custom_call_target="tpu_custom_call" | custom-call | tf_op jit(solution)/shard_map/pallas_call | solution.py:511
  96.7 2.1 %shard_map.103 = (bf16[128,4096]{1,0:T(8,128)(2,1)}, bf16[2,512,512]{2,1,0:T(8,128)(2,1)}, bf16[2,512,512]{2,1,0:T(8,128)(2,1)}, bf16[2,512,512]{2,1,0:T(8,128)(2,1)}) custom-call(bf16[128,4096]{1,0:T(8,128)(2,1)S(1)} %get-tuple-element.6.staged, bf16[6,512,512]{2,1,0:T(8,128)(2,1)S(1)} %get-tuple-element.7.turned), custom_call_target="tpu_custom_call" | custom-call | tf_op jit(solution)/shard_map/pallas_call | solution.py:570

commit v5 on v3

--- a/solution.py
+++ b/solution.py
@@ -108,15 +108,6 @@
         )
     }
 
-    loads["rate"].wait()
-    rate_cols = jnp.transpose(rate_ref[...])
-    loads["value"].wait()
-    for head in range(8):
-        cols = slice(head * WIDTH, (head + 1) * WIDTH)
-        d_own[:, cols] = (-rate_cols[:, head : head + 1] * v_ref[:, cols].astype(jnp.float32)).astype(
-            jnp.bfloat16
-        )
-
     pl.semaphore_wait(barrier, len(greeted))
 
     def exchange(which, src, dst, head):
@@ -135,9 +126,20 @@
             recv_sem=in_recv.at[which, head, n], device_id=sources[n], device_id_type=MESH,
         ).wait_recv()
 
+    exchange(0, k_hbm, k_all, 0)
+    loads["rate"].wait()
+    rate_cols = jnp.transpose(rate_ref[...])
+    loads["value"].wait()
     for head in range(2):
-        exchange(0, k_hbm, k_all, head)
+        for of_group in range(4):
+            index = 2 * of_group + head
+            cols = slice(index * WIDTH, (index + 1) * WIDTH)
+            d_own[:, cols] = (
+                -rate_cols[:, index : index + 1] * v_ref[:, cols].astype(jnp.float32)
+            ).astype(jnp.bfloat16)
         exchange(1, d_own, d_all, head)
+        if head == 0:
+            exchange(0, k_hbm, k_all, 1)
     d_all[slot_rows(0), :] = d_own[:, own_cols]
     for name in ("key", "gate", "up", "down"):
         loads[name].wait()
@@ -320,28 +322,30 @@
 
     for head in range(2):
         gradients(head)
-    for head in range(2):
-        exchange(2, q_hbm, q_all, head)
-    for g in (0, 1, 2, 3):
-        if g == PAIRED:
-            pair_finish()
-        else:
-            reduce_finish(g, 0)
-        reduce_start(g, 0 if g == PAIRED else 1)
-    for g in (0, 1, 2, 3):
-        if g == PAIRED:
-            reduce_finish(g, 0)
-            reduce_start(g, 1)
-        else:
-            reduce_finish(g, 1)
-            last_start(g)
     for g in (0, 1, 3):
+        reduce_finish(g, 0)
+        reduce_start(g, 1)
+    pair_finish()
+    reduce_start(PAIRED, 0)
+    for g in (0, 1):
+        reduce_finish(g, 1)
+        last_start(g)
+    for g in (0, 1):
         renormed(g)
         gather_start(g)
+    reduce_finish(3, 1)
+    last_start(3)
+    reduce_finish(PAIRED, 0)
+    reduce_start(PAIRED, 1)
+    renormed(3)
+    gather_start(3)
+    gather_forward(0)
     reduce_finish(PAIRED, 1)
     renormed(PAIRED)
     gather_start(PAIRED)
-    for g in (0, 1, 3, 2):
+    for head in range(2):
+        exchange(2, q_hbm, q_all, head)
+    for g in (1, 3, PAIRED):
         gather_forward(g)
     share()
     loads["query"].wait()

time: 97.5 us -> 96.6 us (level)
  no operation moved by 1% of the time
where the time goes in v5:
time: 96.6 us
  Pallas kernels  95.9 us (99%)
    pallas_call x1, Pallas kernels, step(): pl.pallas_call(kernel, out_shape=(pltpu.VMEM(queries.shape, bf16), pltpu....  93.2 us
    pallas_call x1, Pallas kernels, step(): pl.pallas_call(finish, out_shape=outs, in_specs=[vmem] * 2, out_specs=[an...  2.69 us

profile of v5, /device:TPU:1, one launch (start us, length us, event | category | flops | bytes accessed | tf_op | source)
XLA Modules:
  0.0 96.6 jit_solution(4526619899679130320)
XLA Ops:
  0.6 93.2 %shard_map.102 = (bf16[128,4096]{1,0:T(8,128)(2,1)S(1)}, bf16[6,512,512]{2,1,0:T(8,128)(2,1)S(1)}) custom-call(bf16[128,4096]{1,0:T(8,128)(2,1)} %q_hbm.1, bf16[128,4096]{1,0:T(8,128)(2,1)} %k_hbm.1, bf16[128,4096]{1,0:T(8,128)(2,1)} %v_hbm.1, f32[8,128]{1,0:T(8,128)} %bitcast.1, bf16[2,512,512]{2,1,0:T(8,128)(2,1)} %gate_hbm.1, ...), custom_call_target="tpu_custom_call" | custom-call | tf_op jit(solution)/shard_map/pallas_call | solution.py:438
  93.9 2.7 %shard_map.103 = (bf16[128,4096]{1,0:T(8,128)(2,1)}, bf16[2,512,512]{2,1,0:T(8,128)(2,1)}, bf16[2,512,512]{2,1,0:T(8,128)(2,1)}, bf16[2,512,512]{2,1,0:T(8,128)(2,1)}) custom-call(bf16[128,4096]{1,0:T(8,128)(2,1)S(1)} %get-tuple-element.6.staged, bf16[6,512,512]{2,1,0:T(8,128)(2,1)S(1)} %get-tuple-element.7.next_t), custom_call_target="tpu_custom_call" | custom-call | tf_op jit(solution)/shard_map/pallas_call | solution.py:494
